TPU v7x, 256 devices: a whole 4x4x8 slice. The times are simulated.
256 devices in a mesh: lat: 8 (over x, y_lo), lon: 32 (over y_hi, z, core).
Axes of the slice: x: 4, y: 4 (y_hi: 2, y_lo: 2; y = y_hi * 2 + y_lo), z: 8, core: 2. Of those that a mesh axis runs over, the one named last changes fastest.
Arguments:
- forcing: float32 [2, 2, 8, 128, 256], P(None, None, None, 'lat', 'lon'), may hold values from -6 to 6
- zonal: float32 [8, 128, 256], P(None, 'lat', 'lon'), may hold values from -0.3 to 0.3
- meridional: float32 [8, 128, 256], P(None, 'lat', 'lon'), may hold values from -0.3 to 0.3
- mixing: float32 [7, 128, 256], P(None, 'lat', 'lon'), may hold values from 0.03 to 0.24
- panel: bfloat16 [32768, 8, 4096], P('lat', None, 'lon'), may hold values from -0.046875 to 0.046875
Outputs:
- adjoint_state: float32 [2, 8, 128, 256], P(None, None, 'lat', 'lon')
- state_grad: float32 [2, 8, 8, 4096], P(None, None, 'lat', 'lon')
- flux_grad: float32 [2, 8, 4096], P(None, 'lat', 'lon')
All inputs are finite; a program needn't handle non-finite values.
Results may differ from a plain program's by a relative error of at most 0.0029.
Values may be sent and summed in bfloat16 or wider, within the bound.
A program may use at most 64 MiB of HBM per device.

v0:
```python
import jax
import jax.numpy as jnp
from jax import lax
from jax.sharding import PartitionSpec as P


def extended(value, sides, width, wrap):
    for axis, dim in sides:
        peers, length = (lax.axis_size(axis), value.shape[dim])
        up = [(i, (i + 1) % peers) for i in range(peers if wrap else peers - 1)]
        down = [(j, i) for i, j in up]
        last = lax.slice_in_dim(value, length - width, length, axis=dim)
        initial = lax.slice_in_dim(value, 0, width, axis=dim)
        before = lax.ppermute(last, axis, up)
        after = lax.ppermute(initial, axis, down)
        value = jnp.concatenate([before, value, after], axis=dim)
    return value


def diffuse(tracer, mixing):
    flow = mixing * (tracer[..., 1:, :, :] - tracer[..., :-1, :, :])
    zeros = jnp.zeros_like(flow[..., :1, :, :])
    return tracer + jnp.concatenate([flow, zeros], -3) - jnp.concatenate([zeros, flow], -3)


def advect_local(tracer, zonal_ext, merid_ext):
    centre = tracer[..., 1:-1, 1:-1]
    out_east = jnp.maximum(zonal_ext[:, 1:-1, 1:-1], 0.0)
    in_west = jnp.minimum(zonal_ext[:, 1:-1, :-2], 0.0)
    out_north = jnp.maximum(merid_ext[:, 1:-1, 1:-1], 0.0)
    in_south = jnp.minimum(merid_ext[:, :-2, 1:-1], 0.0)
    return (
        centre * (1.0 - out_east + in_west - out_north + in_south)
        + tracer[..., 1:-1, 2:] * out_east
        - tracer[..., 1:-1, :-2] * in_west
        + tracer[..., 2:, 1:-1] * out_north
        - tracer[..., :-2, 1:-1] * in_south
    )


def widen(planes):
    widened = extended(planes, (("lon", 2),), 1, True)
    return extended(widened, (("lat", 1),), 1, False)


def row_adder(panel, piece):
    return jnp.einsum("rc,cam->ram", piece, panel, preferred_element_type=jnp.float32)


def precondition(vectors, panel):
    total = row_adder(panel, lax.all_gather(vectors, "lon", axis=1, tiled=True))
    return lax.psum_scatter(total, "lat", scatter_dimension=1, tiled=True)


def shards(forcing, zonal, meridional, mixing, panel):
    levels, band_rows, band_cols = zonal.shape
    cell_count = band_rows * band_cols
    row_index = lax.axis_index("lat") * band_rows + jnp.arange(band_rows, dtype=jnp.int32)
    total_rows = band_rows * lax.axis_size("lat")
    top_mask = (row_index < total_rows - 1).astype(jnp.float32)[None, :, None]
    merid_masked = meridional * top_mask
    started = diffuse(forcing[1], mixing).reshape(2 * levels, band_rows, band_cols)
    widened = widen(jnp.concatenate([started, zonal, merid_masked], 0))
    costate_ext = widened[: 2 * levels].reshape(2, levels, band_rows + 2, band_cols + 2)
    zonal_ext = widened[2 * levels : 3 * levels]
    merid_ext = widened[3 * levels :]
    middle = advect_local(costate_ext, zonal_ext, merid_ext) + forcing[0]
    surface = forcing[1][:, 0] + middle[:, 0]
    flux_vec = surface.reshape(2, cell_count).astype(jnp.bfloat16)
    mixed = diffuse(middle, mixing).reshape(2 * levels, band_rows, band_cols)
    mixed_ext = widen(mixed).reshape(2, levels, band_rows + 2, band_cols + 2)
    adjoint_state = advect_local(mixed_ext, zonal_ext, merid_ext)
    state_vec = adjoint_state.reshape(2 * levels, cell_count).astype(jnp.bfloat16)
    summed = precondition(jnp.concatenate([flux_vec, state_vec], 0), panel)
    flux_grad = summed[:2]
    state_grad = summed[2:].reshape(2, levels, summed.shape[1], summed.shape[2])
    return (adjoint_state, state_grad, flux_grad)


def solution(mesh):
    return jax.shard_map(
        shards,
        mesh=mesh,
        in_specs=(
            P(None, None, None, "lat", "lon"),
            P(None, "lat", "lon"),
            P(None, "lat", "lon"),
            P(None, "lat", "lon"),
            P("lat", None, "lon"),
        ),
        out_specs=(P(None, None, "lat", "lon"), P(None, None, "lat", "lon"), P(None, "lat", "lon")),
        check_vma=False,
    )
```

profile of v0, /device:TPU:32, one launch (start us, length us, event | category | flops | bytes accessed | tf_op | source)
XLA Modules:
  0.0 176.5 jit_solution(2214828230962183955)
XLA Ops:
  7.2 0.8 slice_bitcast_fusion
  8.1 0.8 fusion.13
  8.8 0.9 pad_subtract_fusion.1
  9.7 0.8 broadcast_maximum_fusion
  10.5 0.8 pad_maximum_fusion
  11.4 1.7 collective-permute-start.1
  13.1 0.1 copy.56
  13.2 1.3 collective-permute-done
  14.7 3.5 %collective-permute-start.2 = (f32[32,1,10]{0,1,2:T(1,128)S(1)}, f32[32,1,10]{0,1,2:T(1,128)S(1)}, u32[]{:S(2)}, u32[]{:S(2)}) collective-permute-start(f32[32,1,10]{0,1,2:T(1,128)S(1)} %get-tuple-element.34), channel_id=1, source_target_pairs={{0,32},{32,64},{64,96},{96,128},{128,160},{160,192},{192,224},{1,3... | collective-permute-start | bytes 3848 | tf_op jit(solution)/shard_map/ppermute | solution.py:14
  18.2 1.3 collective-permute-start.3
  19.7 4.0 %collective-permute-done.3 = f32[32,1,10]{0,1,2:T(1,128)S(1)} collective-permute-done((f32[32,1,10]{0,1,2:T(1,128)S(1)}, f32[32,1,10]{0,1,2:T(1,128)S(1)}, u32[]{:S(2)}, u32[]{:S(2)}) %collective-permute-start.3) | collective-permute-done | bytes 1312 | tf_op jit(solution)/shard_map/ppermute | solution.py:15
  23.7 0.1 copy.70
  23.8 0.1 fusion.21
  24.0 0.9 subtract_add_fusion
  24.8 1.0 fusion.8
  25.8 0.8 fusion.12
  26.6 0.6 collective-permute-start.4
  27.2 1.2 collective-permute-start.5
  28.4 1.3 collective-permute-done.4
  29.9 4.2 %collective-permute-start.6 = (f32[16,1,10]{1,2,0:T(8,128)S(1)}, f32[16,1,10]{1,2,0:T(8,128)S(1)}, u32[]{:S(2)}, u32[]{:S(2)}) collective-permute-start(f32[16,1,10]{1,2,0:T(8,128)S(1)} %get-tuple-element.24), channel_id=1, source_target_pairs={{0,32},{32,64},{64,96},{96,128},{128,160},{160,192},{192,224},{1,3... | collective-permute-start | bytes 1928 | tf_op jit(solution)/shard_map/ppermute | solution.py:14
  34.1 1.3 collective-permute-start.7
  35.6 1.3 collective-permute-done.6
  37.0 4.7 %collective-permute-done.7 = f32[16,1,10]{1,2,0:T(8,128)S(1)} collective-permute-done((f32[16,1,10]{1,2,0:T(8,128)S(1)}, f32[16,1,10]{1,2,0:T(8,128)S(1)}, u32[]{:S(2)}, u32[]{:S(2)}) %collective-permute-start.7) | collective-permute-done | bytes 672 | tf_op jit(solution)/shard_map/ppermute | solution.py:15
  41.7 0.2 pad_maximum_fusion.2
  41.9 0.8 fusion.16
  42.7 0.1 convert_element_type.23
  42.9 46.2 %all_gather.3 = bf16[18,4096]{1,0:T(8,128)(2,1)S(1)} all-gather(bf16[18,128]{1,0:T(8,128)(2,1)S(1)} %pad_maximum_fusion.13), channel_id=1, replica_groups=mesh['lat'=8,'lon'=32] {'lon'}, dimensions={1}, use_global_device_ids=true | all-gather | bytes 152064 | tf_op jit(solution)/shard_map/all_gather | solution.py:51
  89.0 5.2 %fusion = f32[18,8,128]{2,0,1:T(8,128)} fusion(bf16[4096,8,128]{2,1,0:T(8,128)(2,1)} %param.9, bf16[18,4096]{1,0:T(8,128)(2,1)S(1)} %all_gather.3), kind=kOutput, calls=%fused_computation | convolution fusion | flops 150994944 | bytes 8609792 | tf_op jit(solution)/shard_map/rc,cam->ram/dot_general | solution.py:47
  94.3 0.6 dynamic-slice
  94.9 71.0 %all-reduce.7.cloned.1.call-done = f32[18,8,128]{2,0,1:T(8,128)} async-done(((f32[18,8,128]{2,0,1:T(8,128)}), f32[18,8,128]{2,0,1:T(8,128)}) %all-reduce.7.cloned.1.call-update) | async-done | bytes 73744
  165.8 1.9 %constant_dynamic-slice_fusion.1 = f32[2,1,128]{2,0,1:T(2,128)} fusion(f32[18,8,128]{2,0,1:T(8,128)} %all-reduce.7.cloned.1.call-done, u32[]{:T(128)} %bitcast.10), kind=kLoop, calls=%fused_computation.56 | loop fusion | bytes 2052 | tf_op jit(solution)/shard_map/slice | solution.py:75
  167.7 1.9 %constant_dynamic-slice_fusion = f32[16,1,128]{2,0,1:T(8,128)} fusion(f32[18,8,128]{2,0,1:T(8,128)} %all-reduce.7.cloned.1.call-done, u32[]{:T(128)S(6)} %convert, u32[]{:T(128)} %bitcast.10), kind=kLoop, calls=%fused_computation.55 | loop fusion | bytes 16392 | tf_op jit(solution)/shard_map/slice | solution.py:76
  (25 shorter events, 1.0 us)
Async XLA Ops:
  7.2 158.7 %all-reduce.7.cloned.1.call-start = ((), (), s32[]{:S(2)}) async-start(), calls=%async_computation | async-start | bytes 196608
  10.5 83.8 %copy-start = (u32[256]{0:T(256)S(1)}, u32[256]{0:T(256)}, u32[]{:S(2)}) copy-start(u32[256]{0:T(256)} %constant.29) | copy-start | bytes 3076
  11.3 3.2 %collective-permute-start = (f32[32,16,1]{1,2,0:T(1,128)S(1)}, f32[32,16,1]{1,2,0:T(1,128)S(1)}, u32[]{:S(2)}, u32[]{:S(2)}) collective-permute-start(f32[32,16,1]{1,2,0:T(1,128)S(1)} %get-tuple-element.26), channel_id=1, source_target_pairs={{0,1},{1,2},{2,3},{3,4},{4,5},{5,6},{6,7},{7,8},{8,9},{9,10},{10,1... | collective-permute-start | bytes 6152 | tf_op jit(solution)/shard_map/ppermute | solution.py:14
  11.4 3.2 %collective-permute-start.1 = (f32[32,16,1]{1,2,0:T(1,128)S(1)}, f32[32,16,1]{1,2,0:T(1,128)S(1)}, u32[]{:S(2)}, u32[]{:S(2)}) collective-permute-start(f32[32,16,1]{1,2,0:T(1,128)S(1)} %get-tuple-element.27), channel_id=1, source_target_pairs={{1,0},{2,1},{3,2},{4,3},{5,4},{6,5},{7,6},{8,7},{9,8},{10,9},{11,1... | collective-permute-start | bytes 6152 | tf_op jit(solution)/shard_map/ppermute | solution.py:15
  14.7 4.8 %collective-permute-start.2 = (f32[32,1,10]{0,1,2:T(1,128)S(1)}, f32[32,1,10]{0,1,2:T(1,128)S(1)}, u32[]{:S(2)}, u32[]{:S(2)}) collective-permute-start(f32[32,1,10]{0,1,2:T(1,128)S(1)} %get-tuple-element.34), channel_id=1, source_target_pairs={{0,32},{32,64},{64,96},{96,128},{128,160},{160,192},{192,224},{1,3... | collective-permute-start | bytes 3848 | tf_op jit(solution)/shard_map/ppermute | solution.py:14
  18.2 5.5 %collective-permute-start.3 = (f32[32,1,10]{0,1,2:T(1,128)S(1)}, f32[32,1,10]{0,1,2:T(1,128)S(1)}, u32[]{:S(2)}, u32[]{:S(2)}) collective-permute-start(f32[32,1,10]{0,1,2:T(1,128)S(1)} %get-tuple-element.33), channel_id=1, source_target_pairs={{32,0},{64,32},{96,64},{128,96},{160,128},{192,160},{224,192},{33,... | collective-permute-start | bytes 3848 | tf_op jit(solution)/shard_map/ppermute | solution.py:15
  26.6 3.2 %collective-permute-start.4 = (f32[16,16,1]{1,2,0:T(1,128)S(1)}, f32[16,16,1]{1,2,0:T(1,128)S(1)}, u32[]{:S(2)}, u32[]{:S(2)}) collective-permute-start(f32[16,16,1]{1,2,0:T(1,128)S(1)} %get-tuple-element.35), channel_id=1, source_target_pairs={{0,1},{1,2},{2,3},{3,4},{4,5},{5,6},{6,7},{7,8},{8,9},{9,10},{10,1... | collective-permute-start | bytes 3080 | tf_op jit(solution)/shard_map/ppermute | solution.py:14
  27.2 2.6 %collective-permute-start.5 = (f32[16,16,1]{1,2,0:T(1,128)S(1)}, f32[16,16,1]{1,2,0:T(1,128)S(1)}, u32[]{:S(2)}, u32[]{:S(2)}) collective-permute-start(f32[16,16,1]{1,2,0:T(1,128)S(1)} %get-tuple-element.36), channel_id=1, source_target_pairs={{1,0},{2,1},{3,2},{4,3},{5,4},{6,5},{7,6},{8,7},{9,8},{10,9},{11,1... | collective-permute-start | bytes 3080 | tf_op jit(solution)/shard_map/ppermute | solution.py:15
  29.9 7.0 %collective-permute-start.6 = (f32[16,1,10]{1,2,0:T(8,128)S(1)}, f32[16,1,10]{1,2,0:T(8,128)S(1)}, u32[]{:S(2)}, u32[]{:S(2)}) collective-permute-start(f32[16,1,10]{1,2,0:T(8,128)S(1)} %get-tuple-element.24), channel_id=1, source_target_pairs={{0,32},{32,64},{64,96},{96,128},{128,160},{160,192},{192,224},{1,3... | collective-permute-start | bytes 1928 | tf_op jit(solution)/shard_map/ppermute | solution.py:14
  34.1 7.6 %collective-permute-start.7 = (f32[16,1,10]{1,2,0:T(8,128)S(1)}, f32[16,1,10]{1,2,0:T(8,128)S(1)}, u32[]{:S(2)}, u32[]{:S(2)}) collective-permute-start(f32[16,1,10]{1,2,0:T(8,128)S(1)} %get-tuple-element.25), channel_id=1, source_target_pairs={{32,0},{64,32},{96,64},{128,96},{160,128},{192,160},{224,192},{33,... | collective-permute-start | bytes 1928 | tf_op jit(solution)/shard_map/ppermute | solution.py:15
Sparse Core Ops, SparseCore 0:
  94.4 71.4 all-reduce.6
where the time goes:
time: 177 us
  waiting for transfers between devices  83.7 us (47%)
  blocking collectives  46.2 us (26%)
  between operations  14.2 us (8%)
  starting transfers between devices  13.9 us (8%)
  other arithmetic  6.9 us (4%)
  local copies, waits for them, and re-layouts  6.38 us (4%)
  matrix products  5.21 us (3%)
    unnamed x2, waiting for transfers between devices  71 us
    all_gather x1, blocking collectives, precondition(): total = row_adder(panel, lax.all_gather(vectors, 'lon', axis=1, tiled=True))  46.2 us
    ppermute x4, waiting for transfers between devices, extended(): after = lax.ppermute(initial, axis, down)  8.77 us
    ppermute x4, starting transfers between devices, extended(): before = lax.ppermute(last, axis, up)  8.36 us
    ppermute x4, starting transfers between devices, extended(): after = lax.ppermute(initial, axis, down)  5.53 us
    dot_general x1, matrix products, row_adder(): jnp.einsum('rc,cam->ram', piece, panel, preferred_element_type=jnp.float32)  5.21 us
    ppermute x4, waiting for transfers between devices, extended(): before = lax.ppermute(last, axis, up)  4 us
  transfers between devices with their start and end apart: 9, of which 6 were waited for; matrix products, arithmetic and copies ran while one was open for 1% of the time, Pallas kernels for 0%

commit v1 on v0

v1 whole, which is shorter than its diff:
```python
import functools

import jax
import jax.numpy as jnp
from jax import lax
from jax.experimental import pallas as pl
from jax.experimental.pallas import tpu as pltpu
from jax.sharding import PartitionSpec as P

MESH = pl.DeviceIdType.MESH
CHUNKS = 8
GROUP = 4


def kernel(n_lat, n_lon, forcing, zonal, merid, mixing, panel, adj_out, state_out, flux_out,
           raw, pan, msg, halo4, halo8, expand, tiles, own, gathered, partial, arrived, adj_buf,
           in_sem, pan_sem, msg_send, msg_recv, gat_send, gat_recv, red_send, red_recv, out_sem):
    lat, lon = lax.axis_index("lat"), lax.axis_index("lon")
    f32, bf16 = jnp.float32, jnp.bfloat16

    def at(dlat, dlon):
        return {"lat": lax.rem(lat + (dlat + n_lat), n_lat), "lon": lax.rem(lon + (dlon + n_lon), n_lon)}

    barrier = pltpu.get_barrier_semaphore()
    corners = [(1, 1), (1, -1), (-1, 1), (-1, -1)]
    for dlat, dlon in corners:
        pl.semaphore_signal(barrier, inc=1, device_id=at(dlat, dlon), device_id_type=MESH)
    for d in range(1, n_lat):
        pl.semaphore_signal(barrier, inc=1, device_id=at(d, 0), device_id_type=MESH)
    for k in range(1, n_lon):
        pl.semaphore_signal(barrier, inc=1, device_id=at(0, k), device_id_type=MESH)

    loads = [
        pltpu.make_async_copy(forcing, raw.at[0:32], in_sem.at[0]),
        pltpu.make_async_copy(zonal, raw.at[32:40], in_sem.at[1]),
        pltpu.make_async_copy(merid, raw.at[40:48], in_sem.at[2]),
        pltpu.make_async_copy(mixing, raw.at[48:55], in_sem.at[3]),
    ]
    for load in loads:
        load.start()
    rows = panel.shape[0] // CHUNKS
    pan_loads = [
        pltpu.make_async_copy(panel.at[i * rows:(i + 1) * rows], pan.at[i * rows:(i + 1) * rows], pan_sem.at[i])
        for i in range(CHUNKS)
    ]
    for load in pan_loads:
        load.start()

    q = lax.broadcasted_iota(jnp.int32, (128, 1024), 0)
    big = lax.broadcasted_iota(jnp.int32, (128, 1024), 1)
    expand[...] = jnp.where((big >> 3) == q, 1.0, 0.0).astype(bf16)
    row16 = lax.broadcasted_iota(jnp.int32, (16, 128), 0)
    lane16 = lax.broadcasted_iota(jnp.int32, (16, 128), 1)
    for a in range(8):
        tiles[a] = jnp.where((lane16 & 7) == a, 1.0, 0.0).astype(bf16)
    tiles[8] = jnp.where((lane16 & 7) == (row16 >> 1), 1.0, 0.0).astype(bf16)

    lane = lax.broadcasted_iota(jnp.int32, (8, 128), 1)
    sub = lax.broadcasted_iota(jnp.int32, (8, 128), 0)
    li = lane & 15
    first_row, last_row = li == 0, li == 15
    first_col, last_col = sub == 0, sub == 7

    for load in loads:
        load.wait()

    def packed(start, count):
        return jnp.concatenate([raw[start + k] for k in range(count)], axis=1)

    zero_level = jnp.zeros((8, 16), f32)
    obs = [packed(0, 8), packed(8, 8)]
    last = [packed(16, 8), packed(24, 8)]
    z = packed(32, 8)
    vm = jnp.where(last_row & (lat == n_lat - 1), 0.0, packed(40, 8))
    mix = jnp.concatenate([raw[48 + k] for k in range(7)] + [zero_level], axis=1)

    def up(x, s):
        return pltpu.roll(x, s % 128, 1)

    def side(x, s):
        return pltpu.roll(x, s % 8, 0)

    def diffuse(x, m):
        flow = m * (up(x, -16) - x)
        return x + flow - up(flow, 16)

    g = [diffuse(x, mix) for x in last]
    mine = g + [z, vm] + obs + [mix]

    def pack_rows(top):
        total = jnp.zeros((8, 128), f32)
        for n, x in enumerate(mine):
            total = jnp.where((li >> 1) == n, up(x, 2 * n - (14 if top else 0)), total)
        return total

    def pack_cols(right, fields):
        total = jnp.zeros((8, 128), f32)
        for n, x in enumerate(fields):
            total = jnp.where((sub >> 1) == n, side(x, 2 * n - (6 if right else 0)), total)
        return total

    msg[0] = pack_rows(True)
    msg[1] = pack_rows(False)
    msg[2] = pack_cols(True, mine[:4])
    msg[3] = pack_cols(True, mine[4:])
    msg[4] = pack_cols(False, mine[:4])
    msg[5] = pack_cols(False, mine[4:])

    pl.semaphore_wait(barrier, (n_lat - 1) + (n_lon - 1) + 4)

    def row_copy(slot, kind, dlat, dlon):
        return pltpu.make_async_remote_copy(
            src_ref=msg.at[kind], dst_ref=halo4.at[slot], send_sem=msg_send.at[slot], recv_sem=msg_recv.at[slot],
            device_id=at(dlat, dlon), device_id_type=MESH)

    def col_copy(slot, kind, dlon):
        return pltpu.make_async_remote_copy(
            src_ref=msg.at[kind:kind + 2], dst_ref=halo8.at[slot], send_sem=msg_send.at[6 + slot],
            recv_sem=msg_recv.at[6 + slot], device_id=at(0, dlon), device_id_type=MESH)

    halos = [
        row_copy(0, 1, -1, 0), row_copy(3, 0, 1, 0), col_copy(0, 4, -1), col_copy(1, 2, 1),
        row_copy(1, 1, -1, -1), row_copy(2, 1, -1, 1), row_copy(4, 0, 1, -1), row_copy(5, 0, 1, 1),
    ]
    for copy in halos:
        copy.start()

    def advect(x, north, south, east, west, c):
        p, nw, qn, ns = c
        return x * (1.0 - p + nw - qn + ns) + east * p - west * nw + north * qn - south * ns

    def coefs(zc, z_west, v, v_south):
        return (jnp.maximum(zc, 0.0), jnp.minimum(z_west, 0.0), jnp.maximum(v, 0.0), jnp.minimum(v_south, 0.0))

    for copy in halos:
        copy.wait_recv()

    def rows_of(slot, n, north):
        return up(halo4[slot], -2 * n if north else 14 - 2 * n)

    def cols_of(slot, n):
        return side(halo8[slot, n // 4], -2 * (n % 4) if slot == 0 else 6 - 2 * (n % 4))

    N = [rows_of(0, n, True) for n in range(7)]
    S = [rows_of(3, n, False) for n in range(7)]
    NE = [rows_of(1, n, True) for n in range(4)]
    NW = [rows_of(2, n, True) for n in range(4)]
    SE = [rows_of(4, n, False) for n in range(4)]
    SW = [rows_of(5, n, False) for n in range(4)]
    E = [cols_of(0, n) for n in range(7)]
    W = [cols_of(1, n) for n in range(7)]

    def north_of(x, xn):
        return jnp.where(last_row, up(xn, 15), up(x, -1))

    def south_of(x, xs):
        return jnp.where(first_row, up(xs, -15), up(x, 1))

    def east_of(x, xe):
        return side(jnp.where(first_col, xe, x), -1)

    def west_of(x, xw):
        return side(jnp.where(last_col, xw, x), 1)

    def middle(me, n_, s_, e_, w_):
        c = coefs(me[2], west_of(me[2], w_[2]), me[3], south_of(me[3], s_[3]))
        return c, [
            advect(me[s], north_of(me[s], n_[s]), south_of(me[s], s_[s]), east_of(me[s], e_[s]), west_of(me[s], w_[s]), c)
            + me[4 + s]
            for s in range(2)
        ]

    coef, mid = middle(mine, N, S, E, W)
    mid_n = middle(N, N, mine, NE, NW)[1]
    mid_s = middle(S, mine, S, SE, SW)[1]
    mid_e = middle(E, NE, SE, E, mine)[1]
    mid_w = middle(W, NW, SW, mine, W)[1]
    surface = [last[s] + mid[s] for s in range(2)]
    adjoint = []
    for s in range(2):
        d = diffuse(mid[s], mix)
        dn, ds = diffuse(mid_n[s], N[6]), diffuse(mid_s[s], S[6])
        de, dw = diffuse(mid_e[s], E[6]), diffuse(mid_w[s], W[6])
        adjoint.append(advect(d, north_of(d, dn), south_of(d, ds), east_of(d, de), west_of(d, dw), coef))

    x = jnp.concatenate([adjoint[0], adjoint[1]], axis=0).astype(bf16)
    y = jnp.dot(x, expand[...], preferred_element_type=f32)
    xs = jnp.concatenate(surface, axis=0).astype(bf16)
    ys = jnp.dot(xs, expand[:, 0:128], preferred_element_type=f32)
    keep = (lax.broadcasted_iota(jnp.int32, (16, 128), 1) & 7) == (lax.broadcasted_iota(jnp.int32, (16, 128), 0) & 7)
    blocks = [jnp.where(keep, y[:, k * 128:(k + 1) * 128], 0.0).astype(bf16) for k in range(8)]
    stacked = jnp.concatenate(blocks, axis=0)
    c_row = lax.broadcasted_iota(jnp.int32, (16, 128), 0)
    c_col = lax.broadcasted_iota(jnp.int32, (16, 128), 1)
    pick = (((c_col >> 4) == (c_row & 7)) & (((c_col >> 3) & 1) == (c_row >> 3)))
    state_vec = jnp.dot(jnp.where(pick, 1.0, 0.0).astype(bf16), stacked, preferred_element_type=f32)
    f_row = lax.broadcasted_iota(jnp.int32, (16, 16), 0)
    f_col = lax.broadcasted_iota(jnp.int32, (16, 16), 1)
    pick_f = jnp.where((f_col >> 3) == (f_row & 1), 1.0, 0.0).astype(bf16)
    flux_vec = jnp.dot(pick_f, jnp.where(keep, ys, 0.0).astype(bf16), preferred_element_type=f32)
    own[...] = jnp.concatenate([state_vec, flux_vec], axis=0).astype(bf16)

    def gather_copy(k):
        return pltpu.make_async_remote_copy(
            src_ref=own, dst_ref=gathered.at[k], send_sem=gat_send.at[k], recv_sem=gat_recv.at[k],
            device_id=at(0, k), device_id_type=MESH)

    for k in range(1, n_lon):
        gather_copy(k).start()

    for s in range(2):
        for k in range(8):
            adj_buf[s * 8 + k] = up(adjoint[s], -16 * k)[:, 0:16]
    adj_copy = pltpu.make_async_copy(adj_buf, adj_out, out_sem.at[0])
    adj_copy.start()

    gathered[0] = own[...]
    for load in pan_loads:
        load.wait()

    def piece(k, acc):
        w = jnp.dot(gathered[k], expand[...], preferred_element_type=f32).astype(bf16)
        left = jnp.concatenate(
            [jnp.concatenate([w[0:16, b * 128:(b + 1) * 128] * tiles[a] for b in range(8)], axis=1) for a in range(8)]
            + [jnp.concatenate([w[16:32, b * 128:(b + 1) * 128] * tiles[8] for b in range(8)], axis=1)], axis=0)
        source = lax.rem(lon - k + n_lon, n_lon)
        right = pan[pl.ds(source * 128, 128)].reshape(1024, 128)
        return acc + jnp.dot(left, right, preferred_element_type=f32)

    acc = piece(0, jnp.zeros((144, 128), f32))
    for k in range(1, GROUP):
        gather_copy(k).wait_recv()
        acc = piece(k, acc)

    def group(i, acc):
        for j in range(GROUP):
            k = i * GROUP + j
            gather_copy(k).wait_recv()
            acc = piece(k, acc)
        return acc

    acc = lax.fori_loop(1, n_lon // GROUP, group, acc)

    for a in range(n_lat):
        partial[a, 0:16] = acc[a * 16:(a + 1) * 16]
        partial[a, 16:18] = acc[128 + 2 * a:130 + 2 * a]

    def reduce_copy(d):
        return pltpu.make_async_remote_copy(
            src_ref=partial.at[lax.rem(lat + d, n_lat)], dst_ref=arrived.at[d - 1], send_sem=red_send.at[d - 1],
            recv_sem=red_recv.at[d - 1], device_id=at(d, 0), device_id_type=MESH)

    for d in range(1, n_lat):
        reduce_copy(d).start()
    for copy in halos:
        copy.wait_send()
    for k in range(1, n_lon):
        gather_copy(k).wait_send()
    total = partial[lat]
    for d in range(1, n_lat):
        reduce_copy(d).wait_recv()
        total = total + arrived[d - 1]
    state_out[...] = total[0:16]
    flux_out[...] = total[16:18]
    for d in range(1, n_lat):
        reduce_copy(d).wait_send()
    adj_copy.wait()


def shards(n_lat, n_lon, forcing, zonal, meridional, mixing, panel):
    def turned(x):
        return jnp.swapaxes(x, -1, -2).reshape((-1, x.shape[-1], x.shape[-2]))

    f32, bf16 = jnp.float32, jnp.bfloat16
    rows = panel.shape[0]
    hbm, vmem = pl.BlockSpec(memory_space=pl.ANY), pl.BlockSpec(memory_space=pltpu.VMEM)
    dma = pltpu.SemaphoreType.DMA
    adj, state, flux = pl.pallas_call(
        functools.partial(kernel, n_lat, n_lon),
        out_shape=(
            jax.ShapeDtypeStruct((16, 8, 16), f32),
            jax.ShapeDtypeStruct((16, 128), f32),
            jax.ShapeDtypeStruct((2, 128), f32),
        ),
        in_specs=[hbm] * 5,
        out_specs=(hbm, vmem, vmem),
        scratch_shapes=[
            pltpu.VMEM((55, 8, 16), f32),
            pltpu.VMEM((rows, 8, 128), bf16),
            pltpu.VMEM((6, 8, 128), f32),
            pltpu.VMEM((6, 8, 128), f32),
            pltpu.VMEM((2, 2, 8, 128), f32),
            pltpu.VMEM((128, 1024), bf16),
            pltpu.VMEM((9, 16, 128), bf16),
            pltpu.VMEM((32, 128), bf16),
            pltpu.VMEM((n_lon, 32, 128), bf16),
            pltpu.VMEM((n_lat, 24, 128), f32),
            pltpu.VMEM((n_lat - 1, 24, 128), f32),
            pltpu.VMEM((16, 8, 16), f32),
            dma((4,)), dma((CHUNKS,)), dma((8,)), dma((8,)), dma((n_lon,)), dma((n_lon,)),
            dma((n_lat - 1,)), dma((n_lat - 1,)), dma((1,)),
        ],
        compiler_params=pltpu.CompilerParams(
            collective_id=0, has_side_effects=True, vmem_limit_bytes=48 * 1024 * 1024),
    )(turned(forcing), turned(zonal), turned(meridional), turned(mixing), panel)
    adjoint = jnp.swapaxes(adj.reshape(2, 8, 8, 16), 2, 3)
    return adjoint, state.reshape(2, 8, 1, 128), flux.reshape(2, 1, 128)


def solution(mesh):
    return jax.shard_map(
        functools.partial(shards, mesh.shape["lat"], mesh.shape["lon"]),
        mesh=mesh,
        in_specs=(
            P(None, None, None, "lat", "lon"),
            P(None, "lat", "lon"),
            P(None, "lat", "lon"),
            P(None, "lat", "lon"),
            P("lat", None, "lon"),
        ),
        out_specs=(P(None, None, "lat", "lon"), P(None, None, "lat", "lon"), P(None, "lat", "lon")),
        check_vma=False,
    )
```

time: 177 us -> 42.2 us (0.24)
  the two profiles are of different devices: /device:TPU:32 before, /device:TPU:1 now
where the time goes in v1:
time: 42.2 us; the launch traced here: 41.9 us
  Pallas kernels  36.3 us (86%)
  local copies, waits for them, and re-layouts  4.95 us (12%)
  between operations  0.65 us (2%)
    pallas_call x1, Pallas kernels, shards(): pl.pallas_call(functools.partial(kernel, n_lat, n_lon), out_shape=(jax.Sh...  36.3 us
    unnamed x11, local copies, waits for them, and re-layouts  4.95 us

profile of v1, /device:TPU:1, one launch (start us, length us, event | category | flops | bytes accessed | tf_op | source)
XLA Modules:
  0.0 41.9 jit_solution(17272411303448854331)
XLA Ops:
  0.6 0.0 copy-start
  0.6 0.9 %copy-done = f32[2,2,8,16,8]{3,4,2,1,0:T(8,128)S(1)} copy-done((f32[2,2,8,16,8]{3,4,2,1,0:T(8,128)S(1)}, f32[2,2,8,16,8]{3,4,2,1,0:T(8,128)}, u32[]{:S(2)}) %copy-start) | copy-done | bytes 16408
  1.5 0.0 copy-start.1
  1.5 0.8 %copy-done.1 = f32[8,16,8]{1,2,0:T(8,128)S(1)} copy-done((f32[8,16,8]{1,2,0:T(8,128)S(1)}, f32[8,16,8]{1,2,0:T(8,128)}, u32[]{:S(2)}) %copy-start.1) | copy-done | bytes 4120
  2.3 0.0 copy-start.2
  2.3 0.8 %copy-done.2 = f32[8,16,8]{1,2,0:T(8,128)S(1)} copy-done((f32[8,16,8]{1,2,0:T(8,128)S(1)}, f32[8,16,8]{1,2,0:T(8,128)}, u32[]{:S(2)}) %copy-start.2) | copy-done | bytes 4120
  3.1 0.0 copy-start.3
  3.1 0.7 %copy-done.3 = f32[7,16,8]{1,2,0:T(8,128)S(1)} copy-done((f32[7,16,8]{1,2,0:T(8,128)S(1)}, f32[7,16,8]{1,2,0:T(8,128)}, u32[]{:S(2)}) %copy-start.3) | copy-done | bytes 3608
  3.8 36.3 %shard_map.76 = (f32[16,8,16]{2,1,0:T(8,128)S(1)}, f32[16,128]{1,0:T(8,128)S(1)}, f32[2,128]{1,0:T(2,128)S(1)}) custom-call(f32[32,8,16]{2,1,0:T(8,128)S(1)} %bitcast.15, f32[8,8,16]{2,1,0:T(8,128)S(1)} %bitcast.17, f32[8,8,16]{2,1,0:T(8,128)S(1)} %bitcast.18, f32[7,8,16]{2,1,0:T(8,128)S(1)} %bitcast.19, bf16[4096,8,128]{2,1,0:T(8,128)(2,1)} %panel.1), custom_call_target="tpu_custom_call" | custom-call | tf_op jit(solution)/shard_map/pallas_call | solution.py:278
  40.1 0.6 %copy.13 = f32[2,8,16,8]{2,3,1,0:T(8,128)} copy(f32[2,8,16,8]{2,3,1,0:T(8,128)S(1)} %bitcast.16) | data formatting | bytes 16384
  40.7 0.6 %copy.14 = f32[2,8,1,128]{3,2,1,0:T(1,128)} copy(f32[2,8,1,128]{3,2,1,0:T(1,128)S(1)} %bitcast.20) | data formatting | bytes 16384
  41.3 0.6 %copy.15 = f32[2,1,128]{2,1,0:T(1,128)} copy(f32[2,1,128]{2,1,0:T(1,128)S(1)} %bitcast.21) | data formatting | bytes 2048
Async XLA Ops:
  0.6 0.9 %copy-start = (f32[2,2,8,16,8]{3,4,2,1,0:T(8,128)S(1)}, f32[2,2,8,16,8]{3,4,2,1,0:T(8,128)}, u32[]{:S(2)}) copy-start(f32[2,2,8,16,8]{3,4,2,1,0:T(8,128)} %param.5) | copy-start | bytes 49156
  1.5 0.8 %copy-start.1 = (f32[8,16,8]{1,2,0:T(8,128)S(1)}, f32[8,16,8]{1,2,0:T(8,128)}, u32[]{:S(2)}) copy-start(f32[8,16,8]{1,2,0:T(8,128)} %param.6) | copy-start | bytes 12292
  2.3 0.8 %copy-start.2 = (f32[8,16,8]{1,2,0:T(8,128)S(1)}, f32[8,16,8]{1,2,0:T(8,128)}, u32[]{:S(2)}) copy-start(f32[8,16,8]{1,2,0:T(8,128)} %param.7) | copy-start | bytes 12292
  3.1 0.7 %copy-start.3 = (f32[7,16,8]{1,2,0:T(8,128)S(1)}, f32[7,16,8]{1,2,0:T(8,128)}, u32[]{:S(2)}) copy-start(f32[7,16,8]{1,2,0:T(8,128)} %param.8) | copy-start | bytes 10756

commit v2 on v1

--- a/solution.py
+++ b/solution.py
@@ -9,11 +9,10 @@
 
 MESH = pl.DeviceIdType.MESH
 CHUNKS = 8
-GROUP = 4
 
 
 def kernel(n_lat, n_lon, forcing, zonal, merid, mixing, panel, adj_out, state_out, flux_out,
-           raw, pan, msg, halo4, halo8, expand, tiles, own, gathered, partial, arrived, adj_buf,
+           raw, pan, msg, halo4, halo8, expand, wide, own, gathered, partial, arrived, adj_buf,
            in_sem, pan_sem, msg_send, msg_recv, gat_send, gat_recv, red_send, red_recv, out_sem):
     lat, lon = lax.axis_index("lat"), lax.axis_index("lon")
     f32, bf16 = jnp.float32, jnp.bfloat16
@@ -49,12 +48,6 @@
     q = lax.broadcasted_iota(jnp.int32, (128, 1024), 0)
     big = lax.broadcasted_iota(jnp.int32, (128, 1024), 1)
     expand[...] = jnp.where((big >> 3) == q, 1.0, 0.0).astype(bf16)
-    row16 = lax.broadcasted_iota(jnp.int32, (16, 128), 0)
-    lane16 = lax.broadcasted_iota(jnp.int32, (16, 128), 1)
-    for a in range(8):
-        tiles[a] = jnp.where((lane16 & 7) == a, 1.0, 0.0).astype(bf16)
-    tiles[8] = jnp.where((lane16 & 7) == (row16 >> 1), 1.0, 0.0).astype(bf16)
-
     lane = lax.broadcasted_iota(jnp.int32, (8, 128), 1)
     sub = lax.broadcasted_iota(jnp.int32, (8, 128), 0)
     li = lane & 15
@@ -125,12 +118,25 @@
     for copy in halos:
         copy.start()
 
+    def relayout(begin, end):
+        for i in range(begin, end):
+            pan_loads[i].wait()
+
+            def turn(j, carry):
+                at_row = i * rows + j * 128
+                wide[pl.ds(at_row, 128), :] = pan[pl.ds(at_row, 128)].reshape(128, 1024)
+                return carry
+
+            lax.fori_loop(0, rows // 128, turn, 0)
+
     def advect(x, north, south, east, west, c):
         p, nw, qn, ns = c
         return x * (1.0 - p + nw - qn + ns) + east * p - west * nw + north * qn - south * ns
 
     def coefs(zc, z_west, v, v_south):
         return (jnp.maximum(zc, 0.0), jnp.minimum(z_west, 0.0), jnp.maximum(v, 0.0), jnp.minimum(v_south, 0.0))
+
+    relayout(0, CHUNKS)
 
     for copy in halos:
         copy.wait_recv()
@@ -202,8 +208,13 @@
 
     def gather_copy(k):
         return pltpu.make_async_remote_copy(
-            src_ref=own, dst_ref=gathered.at[k], send_sem=gat_send.at[k], recv_sem=gat_recv.at[k],
+            src_ref=own, dst_ref=gathered.at[lon], send_sem=gat_send.at[k], recv_sem=gat_recv.at[lon],
             device_id=at(0, k), device_id_type=MESH)
+
+    def gather_wait(l):
+        return pltpu.make_async_remote_copy(
+            src_ref=own, dst_ref=gathered.at[l], send_sem=gat_send.at[0], recv_sem=gat_recv.at[l],
+            device_id=at(0, 1), device_id_type=MESH)
 
     for k in range(1, n_lon):
         gather_copy(k).start()
@@ -214,36 +225,20 @@
     adj_copy = pltpu.make_async_copy(adj_buf, adj_out, out_sem.at[0])
     adj_copy.start()
 
-    gathered[0] = own[...]
-    for load in pan_loads:
-        load.wait()
-
-    def piece(k, acc):
-        w = jnp.dot(gathered[k], expand[...], preferred_element_type=f32).astype(bf16)
-        left = jnp.concatenate(
-            [jnp.concatenate([w[0:16, b * 128:(b + 1) * 128] * tiles[a] for b in range(8)], axis=1) for a in range(8)]
-            + [jnp.concatenate([w[16:32, b * 128:(b + 1) * 128] * tiles[8] for b in range(8)], axis=1)], axis=0)
-        source = lax.rem(lon - k + n_lon, n_lon)
-        right = pan[pl.ds(source * 128, 128)].reshape(1024, 128)
-        return acc + jnp.dot(left, right, preferred_element_type=f32)
-
-    acc = piece(0, jnp.zeros((144, 128), f32))
-    for k in range(1, GROUP):
-        gather_copy(k).wait_recv()
-        acc = piece(k, acc)
-
-    def group(i, acc):
-        for j in range(GROUP):
-            k = i * GROUP + j
-            gather_copy(k).wait_recv()
-            acc = piece(k, acc)
-        return acc
-
-    acc = lax.fori_loop(1, n_lon // GROUP, group, acc)
+    gathered[lon] = own[...]
+    acc = None
+    for pair in range(n_lon // 2):
+        first = pair // 2 * 2 + pair % 2 * (n_lon // 2)
+        for l in (first, first + 1):
+            @pl.when(lon != l)
+            def _():
+                gather_wait(l).wait_recv()
+        left = jnp.concatenate([gathered[first], gathered[first + 1]], axis=1)
+        term = jnp.dot(left, wide[first * 128:(first + 2) * 128, :], preferred_element_type=f32)
+        acc = term if acc is None else acc + term
 
     for a in range(n_lat):
-        partial[a, 0:16] = acc[a * 16:(a + 1) * 16]
-        partial[a, 16:18] = acc[128 + 2 * a:130 + 2 * a]
+        partial[a] = acc[0:24, a * 128:(a + 1) * 128]
 
     def reduce_copy(d):
         return pltpu.make_async_remote_copy(
@@ -273,7 +268,7 @@
 
     f32, bf16 = jnp.float32, jnp.bfloat16
     rows = panel.shape[0]
-    hbm, vmem = pl.BlockSpec(memory_space=pl.ANY), pl.BlockSpec(memory_space=pltpu.VMEM)
+    hbm, vmem = pl.BlockSpec(memory_space=pltpu.HBM), pl.BlockSpec(memory_space=pltpu.VMEM)
     dma = pltpu.SemaphoreType.DMA
     adj, state, flux = pl.pallas_call(
         functools.partial(kernel, n_lat, n_lon),
@@ -291,7 +286,7 @@
             pltpu.VMEM((6, 8, 128), f32),
             pltpu.VMEM((2, 2, 8, 128), f32),
             pltpu.VMEM((128, 1024), bf16),
-            pltpu.VMEM((9, 16, 128), bf16),
+            pltpu.VMEM((rows, 1024), bf16),
             pltpu.VMEM((32, 128), bf16),
             pltpu.VMEM((n_lon, 32, 128), bf16),
             pltpu.VMEM((n_lat, 24, 128), f32),
@@ -301,7 +296,7 @@
             dma((n_lat - 1,)), dma((n_lat - 1,)), dma((1,)),
         ],
         compiler_params=pltpu.CompilerParams(
-            collective_id=0, has_side_effects=True, vmem_limit_bytes=48 * 1024 * 1024),
+            collective_id=0, has_side_effects=True, vmem_limit_bytes=56 * 1024 * 1024),
     )(turned(forcing), turned(zonal), turned(meridional), turned(mixing), panel)
     adjoint = jnp.swapaxes(adj.reshape(2, 8, 8, 16), 2, 3)
     return adjoint, state.reshape(2, 8, 1, 128), flux.reshape(2, 1, 128)

time: 42.2 us -> 35.4 us (0.84)
  Pallas kernels: 36.3 us -> 30.6 us
  local copies, waits for them, and re-layouts: 4.95 us -> 3.99 us
    pallas_call x1, Pallas kernels: 36.3 us -> 30.6 us  [shards(): pl.pallas_call(functools.partial(kernel, n_lat, n_lon), out_shape=(jax.Sh...]
    unnamed x11 -> x3, local copies, waits for them, and re-layouts: 4.95 us -> 3.99 us
where the time goes in v2:
time: 35.4 us; the launch traced here: 35.3 us
  Pallas kernels  30.6 us (86%)
  local copies, waits for them, and re-layouts  3.99 us (11%)
  between operations  0.64 us (2%)
    pallas_call x1, Pallas kernels, shards(): pl.pallas_call(functools.partial(kernel, n_lat, n_lon), out_shape=(jax.Sh...  30.6 us
    unnamed x3, local copies, waits for them, and re-layouts  3.99 us

profile of v2, /device:TPU:1, one launch (start us, length us, event | category | flops | bytes accessed | tf_op | source)
XLA Modules:
  0.0 35.3 jit_solution(1969090288485226435)
XLA Ops:
  0.6 30.6 %shard_map.76 = (f32[16,8,16]{2,1,0:T(8,128)}, f32[16,128]{1,0:T(8,128)}, f32[2,128]{1,0:T(2,128)}) custom-call(f32[32,8,16]{2,1,0:T(8,128)} %bitcast.15, f32[8,8,16]{2,1,0:T(8,128)} %bitcast.17, f32[8,8,16]{2,1,0:T(8,128)} %bitcast.18, f32[7,8,16]{2,1,0:T(8,128)} %bitcast.19, bf16[4096,8,128]{2,1,0:T(8,128)(2,1)} %panel.1), custom_call_target="tpu_custom_call" | custom-call | tf_op jit(solution)/shard_map/pallas_call | solution.py:273
  31.3 1.5 %copy.13 = f32[2,8,16,8]{2,3,1,0:T(8,128)} copy(f32[2,8,16,8]{2,3,1,0:T(8,128)} %bitcast.16) | data formatting | bytes 16384
  32.7 1.3 %copy.14 = f32[2,8,1,128]{3,2,1,0:T(1,128)} copy(f32[2,8,1,128]{3,2,1,0:T(1,128)} %bitcast.20) | data formatting | bytes 16384
  34.0 1.2 %copy.15 = f32[2,1,128]{2,1,0:T(1,128)} copy(f32[2,1,128]{2,1,0:T(1,128)} %bitcast.21) | data formatting | bytes 2048

commit v3 on v2

--- a/solution.py
+++ b/solution.py
@@ -9,11 +9,12 @@
 
 MESH = pl.DeviceIdType.MESH
 CHUNKS = 8
-
-
-def kernel(n_lat, n_lon, forcing, zonal, merid, mixing, panel, adj_out, state_out, flux_out,
-           raw, pan, msg, halo4, halo8, expand, wide, own, gathered, partial, arrived, adj_buf,
-           in_sem, pan_sem, msg_send, msg_recv, gat_send, gat_recv, red_send, red_recv, out_sem):
+LIMIT = 55200
+
+
+def kernel(n_lat, n_lon, forcing, zonal, merid, mixing, panel, adj_out, sum_out,
+           raw, pan, msg, halo4, halo8, expand, wide, own, gathered, partial, arrived,
+           in_sem, pan_sem, msg_send, msg_recv, gat_send, gat_recv, red_send, red_recv):
     lat, lon = lax.axis_index("lat"), lax.axis_index("lon")
     f32, bf16 = jnp.float32, jnp.bfloat16
 
@@ -196,49 +197,58 @@
     keep = (lax.broadcasted_iota(jnp.int32, (16, 128), 1) & 7) == (lax.broadcasted_iota(jnp.int32, (16, 128), 0) & 7)
     blocks = [jnp.where(keep, y[:, k * 128:(k + 1) * 128], 0.0).astype(bf16) for k in range(8)]
     stacked = jnp.concatenate(blocks, axis=0)
-    c_row = lax.broadcasted_iota(jnp.int32, (16, 128), 0)
-    c_col = lax.broadcasted_iota(jnp.int32, (16, 128), 1)
-    pick = (((c_col >> 4) == (c_row & 7)) & (((c_col >> 3) & 1) == (c_row >> 3)))
-    state_vec = jnp.dot(jnp.where(pick, 1.0, 0.0).astype(bf16), stacked, preferred_element_type=f32)
-    f_row = lax.broadcasted_iota(jnp.int32, (16, 16), 0)
-    f_col = lax.broadcasted_iota(jnp.int32, (16, 16), 1)
-    pick_f = jnp.where((f_col >> 3) == (f_row & 1), 1.0, 0.0).astype(bf16)
-    flux_vec = jnp.dot(pick_f, jnp.where(keep, ys, 0.0).astype(bf16), preferred_element_type=f32)
-    own[...] = jnp.concatenate([state_vec, flux_vec], axis=0).astype(bf16)
-
-    def gather_copy(k):
+    c_row = lax.broadcasted_iota(jnp.int32, (18, 128), 0)
+    c_col = lax.broadcasted_iota(jnp.int32, (18, 128), 1)
+    pick = (c_row < 16) & ((c_col >> 4) == (c_row & 7)) & (((c_col >> 3) & 1) == (c_row >> 3))
+    f_row = lax.broadcasted_iota(jnp.int32, (18, 16), 0)
+    f_col = lax.broadcasted_iota(jnp.int32, (18, 16), 1)
+    pick_f = (f_col >> 3) == (f_row - 16)
+    vec = jnp.dot(jnp.where(pick, 1.0, 0.0).astype(bf16), stacked, preferred_element_type=f32)
+    vec = vec + jnp.dot(
+        jnp.where(pick_f, 1.0, 0.0).astype(bf16), jnp.where(keep, ys, 0.0).astype(bf16), preferred_element_type=f32)
+    own[...] = vec.astype(bf16)
+
+    half = n_lon // 2
+    core, ring, column = lax.rem(lon, 2), lax.rem(lon // 2, half // 2), lon // half
+
+    def other(dz, dy):
+        return lax.rem(column + dy, 2) * half + lax.rem(ring + dz, half // 2) * 2 + core
+
+    mate = lon + 1 - 2 * core
+    peers = [(dz, dy) for dz in range(half // 2) for dy in range(2) if dz + dy > 0]
+    peers = peers[1:] + peers[:1]
+
+    def piece_copy(source, slot, send, target):
         return pltpu.make_async_remote_copy(
-            src_ref=own, dst_ref=gathered.at[lon], send_sem=gat_send.at[k], recv_sem=gat_recv.at[lon],
-            device_id=at(0, k), device_id_type=MESH)
-
-    def gather_wait(l):
-        return pltpu.make_async_remote_copy(
-            src_ref=own, dst_ref=gathered.at[l], send_sem=gat_send.at[0], recv_sem=gat_recv.at[l],
-            device_id=at(0, 1), device_id_type=MESH)
-
-    for k in range(1, n_lon):
-        gather_copy(k).start()
-
+            src_ref=source, dst_ref=gathered.at[slot], send_sem=gat_send.at[send], recv_sem=gat_recv.at[slot],
+            device_id={"lat": lat, "lon": target}, device_id_type=MESH)
+
+    sends = [piece_copy(own, lon, 0, mate)] + [piece_copy(own, lon, 1 + i, other(*d)) for i, d in enumerate(peers)]
+    for copy in sends:
+        copy.start()
+    keep_own = pltpu.make_async_copy(own, gathered.at[lon], gat_send.at[n_lon - 1])
+    keep_own.start()
     for s in range(2):
-        for k in range(8):
-            adj_buf[s * 8 + k] = up(adjoint[s], -16 * k)[:, 0:16]
-    adj_copy = pltpu.make_async_copy(adj_buf, adj_out, out_sem.at[0])
-    adj_copy.start()
-
-    gathered[lon] = own[...]
+        adj_out[s] = adjoint[s]
+
+    for i, d in enumerate(peers):
+        slot = other(*d)
+        piece_copy(own, slot, 0, mate).wait_recv()
+        copy = piece_copy(gathered.at[slot], slot, half + i, mate)
+        copy.start()
+        sends.append(copy)
+
+    keep_own.wait()
     acc = None
-    for pair in range(n_lon // 2):
-        first = pair // 2 * 2 + pair % 2 * (n_lon // 2)
-        for l in (first, first + 1):
-            @pl.when(lon != l)
-            def _():
-                gather_wait(l).wait_recv()
+    for pair in range(half):
+        first = pair // 2 * 2 + pair % 2 * half
+        piece_copy(own, first + 1 - core, 0, mate).wait_recv()
         left = jnp.concatenate([gathered[first], gathered[first + 1]], axis=1)
         term = jnp.dot(left, wide[first * 128:(first + 2) * 128, :], preferred_element_type=f32)
         acc = term if acc is None else acc + term
 
     for a in range(n_lat):
-        partial[a] = acc[0:24, a * 128:(a + 1) * 128]
+        partial[a] = acc[:, a * 128:(a + 1) * 128]
 
     def reduce_copy(d):
         return pltpu.make_async_remote_copy(
@@ -247,19 +257,23 @@
 
     for d in range(1, n_lat):
         reduce_copy(d).start()
-    for copy in halos:
+    for copy in halos + sends:
         copy.wait_send()
-    for k in range(1, n_lon):
-        gather_copy(k).wait_send()
     total = partial[lat]
     for d in range(1, n_lat):
         reduce_copy(d).wait_recv()
         total = total + arrived[d - 1]
+    sum_out[...] = total
+    for d in range(1, n_lat):
+        reduce_copy(d).wait_send()
+
+
+def finish(adj, total, adj_out, state_out, flux_out):
+    for s in range(2):
+        for k in range(8):
+            adj_out[s * 8 + k] = pltpu.roll(adj[s], (-16 * k) % 128, 1)[:, 0:16]
     state_out[...] = total[0:16]
     flux_out[...] = total[16:18]
-    for d in range(1, n_lat):
-        reduce_copy(d).wait_send()
-    adj_copy.wait()
 
 
 def shards(n_lat, n_lon, forcing, zonal, meridional, mixing, panel):
@@ -270,15 +284,11 @@
     rows = panel.shape[0]
     hbm, vmem = pl.BlockSpec(memory_space=pltpu.HBM), pl.BlockSpec(memory_space=pltpu.VMEM)
     dma = pltpu.SemaphoreType.DMA
-    adj, state, flux = pl.pallas_call(
+    adj, total = pl.pallas_call(
         functools.partial(kernel, n_lat, n_lon),
-        out_shape=(
-            jax.ShapeDtypeStruct((16, 8, 16), f32),
-            jax.ShapeDtypeStruct((16, 128), f32),
-            jax.ShapeDtypeStruct((2, 128), f32),
-        ),
+        out_shape=(jax.ShapeDtypeStruct((2, 8, 128), f32), jax.ShapeDtypeStruct((18, 128), f32)),
         in_specs=[hbm] * 5,
-        out_specs=(hbm, vmem, vmem),
+        out_specs=(vmem, vmem),
         scratch_shapes=[
             pltpu.VMEM((55, 8, 16), f32),
             pltpu.VMEM((rows, 8, 128), bf16),
@@ -287,17 +297,27 @@
             pltpu.VMEM((2, 2, 8, 128), f32),
             pltpu.VMEM((128, 1024), bf16),
             pltpu.VMEM((rows, 1024), bf16),
-            pltpu.VMEM((32, 128), bf16),
-            pltpu.VMEM((n_lon, 32, 128), bf16),
-            pltpu.VMEM((n_lat, 24, 128), f32),
-            pltpu.VMEM((n_lat - 1, 24, 128), f32),
-            pltpu.VMEM((16, 8, 16), f32),
+            pltpu.VMEM((18, 128), bf16),
+            pltpu.VMEM((n_lon, 18, 128), bf16),
+            pltpu.VMEM((n_lat, 18, 128), f32),
+            pltpu.VMEM((n_lat - 1, 18, 128), f32),
             dma((4,)), dma((CHUNKS,)), dma((8,)), dma((8,)), dma((n_lon,)), dma((n_lon,)),
-            dma((n_lat - 1,)), dma((n_lat - 1,)), dma((1,)),
+            dma((n_lat - 1,)), dma((n_lat - 1,)),
         ],
         compiler_params=pltpu.CompilerParams(
-            collective_id=0, has_side_effects=True, vmem_limit_bytes=56 * 1024 * 1024),
+            collective_id=0, has_side_effects=True, vmem_limit_bytes=LIMIT * 1024),
     )(turned(forcing), turned(zonal), turned(meridional), turned(mixing), panel)
+    adj, state, flux = pl.pallas_call(
+        finish,
+        out_shape=(
+            jax.ShapeDtypeStruct((16, 8, 16), f32),
+            jax.ShapeDtypeStruct((16, 128), f32),
+            jax.ShapeDtypeStruct((2, 128), f32),
+        ),
+        in_specs=[vmem] * 2,
+        out_specs=(vmem,) * 3,
+        compiler_params=pltpu.CompilerParams(vmem_limit_bytes=1024 * 1024),
+    )(adj, total)
     adjoint = jnp.swapaxes(adj.reshape(2, 8, 8, 16), 2, 3)
     return adjoint, state.reshape(2, 8, 1, 128), flux.reshape(2, 1, 128)
 

time: 35.4 us -> 30.8 us (0.87)
  local copies, waits for them, and re-layouts: 3.99 us -> 0 us
  Pallas kernels: 30.6 us -> 30.1 us
    unnamed x3 -> x0, local copies, waits for them, and re-layouts: 3.99 us -> none
    pallas_call x1, Pallas kernels: 30.6 us -> 29.3 us  [shards(): pl.pallas_call(functools.partial(kernel, n_lat, n_lon), out_shape=(jax.Sh...]
    pallas_call x0 -> x1, Pallas kernels: none -> 0.71 us  [shards(): pl.pallas_call(finish, out_shape=(jax.ShapeDtypeStruct((16, 8, 16), f32),...]
where the time goes in v3:
time: 30.8 us; the launch traced here: 30.7 us
  Pallas kernels  30.1 us (98%)
  between operations  0.64 us (2%)
    pallas_call x1, Pallas kernels, shards(): pl.pallas_call(functools.partial(kernel, n_lat, n_lon), out_shape=(jax.Sh...  29.3 us
    pallas_call x1, Pallas kernels, shards(): pl.pallas_call(finish, out_shape=(jax.ShapeDtypeStruct((16, 8, 16), f32),...  0.71 us

profile of v3, /device:TPU:1, one launch (start us, length us, event | category | flops | bytes accessed | tf_op | source)
XLA Modules:
  0.0 30.7 jit_solution(4785887902524896792)
XLA Ops:
  0.6 29.3 %shard_map.76 = (f32[2,8,128]{2,1,0:T(8,128)S(1)}, f32[18,128]{1,0:T(8,128)S(1)}) custom-call(f32[32,8,16]{2,1,0:T(8,128)} %bitcast.15, f32[8,8,16]{2,1,0:T(8,128)} %bitcast.16, f32[8,8,16]{2,1,0:T(8,128)} %bitcast.17, f32[7,8,16]{2,1,0:T(8,128)} %bitcast.18, bf16[4096,8,128]{2,1,0:T(8,128)(2,1)} %panel.1), custom_call_target="tpu_custom_call" | custom-call | tf_op jit(solution)/shard_map/pallas_call | solution.py:287
  30.0 0.7 %shard_map.77 = (f32[16,8,16]{2,1,0:T(8,128)}, f32[16,128]{1,0:T(8,128)}, f32[2,128]{1,0:T(2,128)}) custom-call(f32[2,8,128]{2,1,0:T(8,128)S(1)} %get-tuple-element.8.adj, f32[18,128]{1,0:T(8,128)S(1)} %get-tuple-element.9.total), custom_call_target="tpu_custom_call" | custom-call | tf_op jit(solution)/shard_map/pallas_call | solution.py:310

commit v4 on v3

--- a/solution.py
+++ b/solution.py
@@ -21,14 +21,26 @@
     def at(dlat, dlon):
         return {"lat": lax.rem(lat + (dlat + n_lat), n_lat), "lon": lax.rem(lon + (dlon + n_lon), n_lon)}
 
+    half = n_lon // 2
+    core, ring, column = lax.rem(lon, 2), lax.rem(lon // 2, half // 2), lon // half
+
+    def other(dz, dy):
+        return lax.rem(column + dy, 2) * half + lax.rem(ring + dz, half // 2) * 2 + core
+
+    mate = lon + 1 - 2 * core
+    peers = [(dz, dy) for dz in range(half // 2) for dy in range(2) if dz + dy > 0]
+    peers = peers[1:] + peers[:1]
+
     barrier = pltpu.get_barrier_semaphore()
     corners = [(1, 1), (1, -1), (-1, 1), (-1, -1)]
     for dlat, dlon in corners:
         pl.semaphore_signal(barrier, inc=1, device_id=at(dlat, dlon), device_id_type=MESH)
     for d in range(1, n_lat):
         pl.semaphore_signal(barrier, inc=1, device_id=at(d, 0), device_id_type=MESH)
-    for k in range(1, n_lon):
-        pl.semaphore_signal(barrier, inc=1, device_id=at(0, k), device_id_type=MESH)
+    for target in (lon + 1 - 2 * core, lax.rem(lon + 2 * core - 1 + n_lon, n_lon)):
+        pl.semaphore_signal(barrier, inc=1, device_id={"lat": lat, "lon": target}, device_id_type=MESH)
+    for dz, dy in peers:
+        pl.semaphore_signal(barrier, inc=1, device_id={"lat": lat, "lon": other(dz, dy)}, device_id_type=MESH)
 
     loads = [
         pltpu.make_async_copy(forcing, raw.at[0:32], in_sem.at[0]),
@@ -100,7 +112,7 @@
     msg[4] = pack_cols(False, mine[:4])
     msg[5] = pack_cols(False, mine[4:])
 
-    pl.semaphore_wait(barrier, (n_lat - 1) + (n_lon - 1) + 4)
+    pl.semaphore_wait(barrier, (n_lat - 1) + (half + 1) + 4)
 
     def row_copy(slot, kind, dlat, dlon):
         return pltpu.make_async_remote_copy(
@@ -208,22 +220,18 @@
         jnp.where(pick_f, 1.0, 0.0).astype(bf16), jnp.where(keep, ys, 0.0).astype(bf16), preferred_element_type=f32)
     own[...] = vec.astype(bf16)
 
-    half = n_lon // 2
-    core, ring, column = lax.rem(lon, 2), lax.rem(lon // 2, half // 2), lon // half
-
-    def other(dz, dy):
-        return lax.rem(column + dy, 2) * half + lax.rem(ring + dz, half // 2) * 2 + core
-
-    mate = lon + 1 - 2 * core
-    peers = [(dz, dy) for dz in range(half // 2) for dy in range(2) if dz + dy > 0]
-    peers = peers[1:] + peers[:1]
-
     def piece_copy(source, slot, send, target):
         return pltpu.make_async_remote_copy(
             src_ref=source, dst_ref=gathered.at[slot], send_sem=gat_send.at[send], recv_sem=gat_recv.at[slot],
             device_id={"lat": lat, "lon": target}, device_id_type=MESH)
 
-    sends = [piece_copy(own, lon, 0, mate)] + [piece_copy(own, lon, 1 + i, other(*d)) for i, d in enumerate(peers)]
+    near = [d for d in peers if d[0] == 0]
+    far = [d for d in peers if d not in near]
+    targets = [mate]
+    for d in near:
+        targets += [other(*d), other(*d) + 1 - 2 * core]
+    targets += [other(*d) for d in far]
+    sends = [piece_copy(own, lon, i, target) for i, target in enumerate(targets)]
     for copy in sends:
         copy.start()
     keep_own = pltpu.make_async_copy(own, gathered.at[lon], gat_send.at[n_lon - 1])
@@ -231,12 +239,14 @@
     for s in range(2):
         adj_out[s] = adjoint[s]
 
-    for i, d in enumerate(peers):
+    for d in far:
         slot = other(*d)
         piece_copy(own, slot, 0, mate).wait_recv()
-        copy = piece_copy(gathered.at[slot], slot, half + i, mate)
+        copy = piece_copy(gathered.at[slot], slot, len(sends), mate)
         copy.start()
         sends.append(copy)
+    for d in near:
+        piece_copy(own, other(*d), 0, mate).wait_recv()
 
     keep_own.wait()
     acc = None

time: 30.8 us -> 29.7 us (0.964)
  Pallas kernels: 30.1 us -> 28.9 us
    pallas_call x1, Pallas kernels: 29.3 us -> 28.2 us  [shards(): pl.pallas_call(functools.partial(kernel, n_lat, n_lon), out_shape=(jax.Sh...]
where the time goes in v4:
time: 29.7 us; the launch traced here: 29.6 us
  Pallas kernels  28.9 us (97%)
  between operations  0.64 us (2%)
    pallas_call x1, Pallas kernels, shards(): pl.pallas_call(functools.partial(kernel, n_lat, n_lon), out_shape=(jax.Sh...  28.2 us
    pallas_call x1, Pallas kernels, shards(): pl.pallas_call(finish, out_shape=(jax.ShapeDtypeStruct((16, 8, 16), f32),...  0.71 us

profile of v4, /device:TPU:1, one launch (start us, length us, event | category | flops | bytes accessed | tf_op | source)
XLA Modules:
  0.0 29.6 jit_solution(17607337427247080397)
XLA Ops:
  0.6 28.2 %shard_map.76 = (f32[2,8,128]{2,1,0:T(8,128)S(1)}, f32[18,128]{1,0:T(8,128)S(1)}) custom-call(f32[32,8,16]{2,1,0:T(8,128)} %bitcast.15, f32[8,8,16]{2,1,0:T(8,128)} %bitcast.16, f32[8,8,16]{2,1,0:T(8,128)} %bitcast.17, f32[7,8,16]{2,1,0:T(8,128)} %bitcast.18, bf16[4096,8,128]{2,1,0:T(8,128)(2,1)} %panel.1), custom_call_target="tpu_custom_call" | custom-call | tf_op jit(solution)/shard_map/pallas_call | solution.py:297
  28.9 0.7 %shard_map.77 = (f32[16,8,16]{2,1,0:T(8,128)}, f32[16,128]{1,0:T(8,128)}, f32[2,128]{1,0:T(2,128)}) custom-call(f32[2,8,128]{2,1,0:T(8,128)S(1)} %get-tuple-element.8.adj, f32[18,128]{1,0:T(8,128)S(1)} %get-tuple-element.9.total), custom_call_target="tpu_custom_call" | custom-call | tf_op jit(solution)/shard_map/pallas_call | solution.py:320

commit v5 on v4

--- a/solution.py
+++ b/solution.py
@@ -28,8 +28,7 @@
         return lax.rem(column + dy, 2) * half + lax.rem(ring + dz, half // 2) * 2 + core
 
     mate = lon + 1 - 2 * core
-    peers = [(dz, dy) for dz in range(half // 2) for dy in range(2) if dz + dy > 0]
-    peers = peers[1:] + peers[:1]
+    peers = [(dz, dy) for dz in range(half // 2) for dy in (1, 0) if dz + dy > 0]
 
     barrier = pltpu.get_barrier_semaphore()
     corners = [(1, 1), (1, -1), (-1, 1), (-1, -1)]
@@ -125,8 +124,8 @@
             recv_sem=msg_recv.at[6 + slot], device_id=at(0, dlon), device_id_type=MESH)
 
     halos = [
+        row_copy(1, 1, -1, -1), row_copy(2, 1, -1, 1), row_copy(4, 0, 1, -1), row_copy(5, 0, 1, 1),
         row_copy(0, 1, -1, 0), row_copy(3, 0, 1, 0), col_copy(0, 4, -1), col_copy(1, 2, 1),
-        row_copy(1, 1, -1, -1), row_copy(2, 1, -1, 1), row_copy(4, 0, 1, -1), row_copy(5, 0, 1, 1),
     ]
     for copy in halos:
         copy.start()
@@ -227,10 +226,11 @@
 
     near = [d for d in peers if d[0] == 0]
     far = [d for d in peers if d not in near]
+    by_far = sorted(far, key=lambda d: -min(d[0], half // 2 - d[0]))
     targets = [mate]
     for d in near:
         targets += [other(*d), other(*d) + 1 - 2 * core]
-    targets += [other(*d) for d in far]
+    targets += [other(*d) for d in by_far]
     sends = [piece_copy(own, lon, i, target) for i, target in enumerate(targets)]
     for copy in sends:
         copy.start()
@@ -265,7 +265,7 @@
             src_ref=partial.at[lax.rem(lat + d, n_lat)], dst_ref=arrived.at[d - 1], send_sem=red_send.at[d - 1],
             recv_sem=red_recv.at[d - 1], device_id=at(d, 0), device_id_type=MESH)
 
-    for d in range(1, n_lat):
+    for d in sorted(range(1, n_lat), key=lambda d: -min(d, n_lat - d)):
         reduce_copy(d).start()
     for copy in halos + sends:
         copy.wait_send()

time: 29.7 us -> 29.2 us (0.983)
  Pallas kernels: 28.9 us -> 28.5 us
    pallas_call x1, Pallas kernels: 28.2 us -> 27.8 us  [shards(): pl.pallas_call(functools.partial(kernel, n_lat, n_lon), out_shape=(jax.Sh...]
where the time goes in v5:
time: 29.2 us; the launch traced here: 29.1 us
  Pallas kernels  28.5 us (98%)
  between operations  0.64 us (2%)
    pallas_call x1, Pallas kernels, shards(): pl.pallas_call(functools.partial(kernel, n_lat, n_lon), out_shape=(jax.Sh...  27.8 us
    pallas_call x1, Pallas kernels, shards(): pl.pallas_call(finish, out_shape=(jax.ShapeDtypeStruct((16, 8, 16), f32),...  0.71 us

profile of v5, /device:TPU:1, one launch (start us, length us, event | category | flops | bytes accessed | tf_op | source)
XLA Modules:
  0.0 29.1 jit_solution(14195077974168234118)
XLA Ops:
  0.6 27.8 %shard_map.76 = (f32[2,8,128]{2,1,0:T(8,128)S(1)}, f32[18,128]{1,0:T(8,128)S(1)}) custom-call(f32[32,8,16]{2,1,0:T(8,128)} %bitcast.15, f32[8,8,16]{2,1,0:T(8,128)} %bitcast.16, f32[8,8,16]{2,1,0:T(8,128)} %bitcast.17, f32[7,8,16]{2,1,0:T(8,128)} %bitcast.18, bf16[4096,8,128]{2,1,0:T(8,128)(2,1)} %panel.1), custom_call_target="tpu_custom_call" | custom-call | tf_op jit(solution)/shard_map/pallas_call | solution.py:297
  28.4 0.7 %shard_map.77 = (f32[16,8,16]{2,1,0:T(8,128)}, f32[16,128]{1,0:T(8,128)}, f32[2,128]{1,0:T(2,128)}) custom-call(f32[2,8,128]{2,1,0:T(8,128)S(1)} %get-tuple-element.8.adj, f32[18,128]{1,0:T(8,128)S(1)} %get-tuple-element.9.total), custom_call_target="tpu_custom_call" | custom-call | tf_op jit(solution)/shard_map/pallas_call | solution.py:320
